TPU v7x, 128 devices: a whole 4x4x4 slice. The times are simulated.
128 devices in a mesh: grp: 8 (over x, core), dev: 16 (over y, z).
Axes of the slice: x: 4, y: 4, z: 4, core: 2. Of those that a mesh axis runs over, the one named last changes fastest.
Arguments:
- emission: float32 [64, 524288], P(None, ('grp', 'dev')), may hold values from 0.2 to 2
- positions: float32 [3, 524288], P(None, ('grp', 'dev')), may hold values from -5 to 5
- normals: float32 [3, 524288], P(None, ('grp', 'dev')), may hold values from -3 to 3
- areas: float32 [524288], P(('grp', 'dev')), may hold values from 0.5 to 4
- material: int32 [524288], P(('grp', 'dev')), may hold values from 0 to 15
- reflect: float32 [64, 16], replicated, may hold values from 0.2 to 0.8
- pair_local: int32 [16384], P(('grp', 'dev')), may hold values from 0 to 31
- pair_device: int32 [16384, 1], P(('grp', 'dev')), may hold values from 0 to 127; in each aligned block of 128 rows (0 to 127, 128 to 255, ...) at most 2 rows name the same one
- pair_block: int32 [16384], P(('grp', 'dev')), may hold values from 0 to 31
Outputs:
- radiosity: float32 [64, 524288], P(None, ('grp', 'dev'))
Inputs may be any that keep to these rules, and one draw needn't show every extreme that they name: `pair_device`: among the 128 pairs of one device, at most 2 name the same device; some device's pairs name one device exactly 2 times.
All inputs are finite; a program needn't handle non-finite values.
Results may differ from a plain program's by a relative error of at most 0.00055.
Values may be sent and summed in bfloat16 or wider, within the bound.
A program may use at most 128 MiB of HBM per device.

v0:
```python
import math

import jax
import jax.numpy as jnp
import numpy as np
from jax import lax
from jax.experimental import pallas as pl
from jax.experimental.pallas import tpu as pltpu
from jax.sharding import PartitionSpec as P

BLK = 128
SWEEPS = 2
AXES = ("grp", "dev")
DEVICES = 128
BLOCKS = 32
BANDS = 64
RANKS = 16
PIECES = 4
RELAYS = RANKS * PIECES
ROWS = 64 // PIECES
HALVES = 2
PLACES = DEVICES // HALVES
FEATURES = 64
MISC = 32
MESH = pl.DeviceIdType.MESH
softening = 0.5


def view_tile(near, far):
    distance_sq = softening
    facing_near = 0.0
    facing_far = 0.0
    for axis_index in range(3):
        offset = far[:, axis_index, None, :] - near[:, axis_index, :, None]
        distance_sq = distance_sq + offset * offset
        facing_near = facing_near + near[:, 3 + axis_index, :, None] * offset
        facing_far = facing_far - far[:, 3 + axis_index, None, :] * offset
    return (
        jnp.maximum(facing_near, 0.0)
        * jnp.maximum(facing_far, 0.0)
        / (math.pi * distance_sq * distance_sq)
    )


def general(
    emission, positions, normals, areas, material, reflect, pair_local, pair_device, pair_block
):
    band_count, patch_count = emission.shape
    local_blocks = patch_count // BLK
    device_count = lax.axis_size(("grp", "dev"))
    pair_count = pair_local.shape[0]
    capacity = max(2, (2 * pair_count + device_count - 1) // device_count)
    slot_total = device_count * capacity
    target = pair_device[:, 0]
    target_hot = (target[:, None] == jnp.arange(device_count, dtype=jnp.int32)[None, :]).astype(
        jnp.int32
    )
    earlier = jnp.cumsum(target_hot, 0) - target_hot
    slot_index = target * capacity + jnp.sum(earlier * target_hot, 1)
    wanted = jnp.zeros((slot_total,), jnp.int32).at[slot_index].set(pair_block)
    asked_for = lax.all_to_all(wanted, ("grp", "dev"), split_axis=0, concat_axis=0, tiled=True)
    geometry = jnp.concatenate([positions, normals, areas[None, :]], 0)
    geometry = geometry.reshape(7, local_blocks, BLK).transpose(1, 0, 2)
    lent_geometry = geometry[asked_for]
    served = lax.all_to_all(lent_geometry, ("grp", "dev"), split_axis=0, concat_axis=0, tiled=True)
    far_geometry = served[slot_index]
    near_geometry = geometry[pair_local]
    block_ids = jnp.arange(local_blocks, dtype=jnp.int32)
    local_hot = (pair_local[:, None] == block_ids[None, :]).astype(jnp.float32)
    asked_hot = (asked_for[:, None] == block_ids[None, :]).astype(jnp.float32)
    class_hot = (
        jnp.arange(reflect.shape[1], dtype=jnp.int32)[:, None] == material[None, :]
    ).astype(jnp.float32)
    albedo = jnp.dot(reflect, class_hot, precision=lax.Precision.HIGHEST)
    albedo = albedo.reshape(band_count, local_blocks, BLK).transpose(1, 0, 2)
    source = emission.reshape(band_count, local_blocks, BLK).transpose(1, 0, 2)
    area_blocks = geometry[:, 6, :]
    current = source
    for sweep_index in range(SWEEPS):
        scaled = (current * area_blocks[:, None, :]).astype(jnp.bfloat16)
        lent_values = scaled[asked_for]
        kernel = view_tile(near_geometry, far_geometry).astype(jnp.bfloat16)
        incoming = lax.all_to_all(
            lent_values, ("grp", "dev"), split_axis=0, concat_axis=0, tiled=True
        )
        to_near = jnp.einsum(
            "pnj,pij->pni", incoming[slot_index], kernel, preferred_element_type=jnp.float32
        )
        to_far = jnp.einsum(
            "pni,pij->pnj", scaled[pair_local], kernel, preferred_element_type=jnp.float32
        )
        replies = jnp.zeros((slot_total, band_count, BLK), jnp.float32).at[slot_index].set(to_far)
        returned = lax.all_to_all(replies, ("grp", "dev"), split_axis=0, concat_axis=0, tiled=True)
        gathered = jnp.einsum("pb,pnk->bnk", local_hot, to_near, precision=lax.Precision.HIGHEST)
        gathered = gathered + jnp.einsum(
            "sb,snk->bnk", asked_hot, returned, precision=lax.Precision.HIGHEST
        )
        current = source + albedo * gathered
    return current.transpose(1, 0, 2).reshape(band_count, patch_count)


def torus_order():
    seen = set()
    groups = []
    for dx in range(4):
        for dy in range(4):
            for dz in range(4):
                for core in range(2):
                    group = []
                    for x, y, z in ((dx, dy, dz), (dy, dz, dx), (dz, dx, dy)):
                        for step in ((x, core, y, z), (-x % 4, core, -y % 4, -z % 4)):
                            if step not in seen and any(step):
                                seen.add(step)
                                group.append(step)
                    if group:
                        groups.append(group)
    groups.sort(key=lambda group: sum(min(v, 4 - v) for v in group[0][:1] + group[0][2:]))
    return [step for group in groups for step in group]


ORDER = torus_order()
PEERS = len(ORDER)


def peer(grp, dev, step):
    x, core, y, z = step
    return (
        lax.rem(grp // 2 + x, 4) * 2 + lax.rem(lax.rem(grp, 2) + core, 2),
        lax.rem(dev // 4 + y, 4) * 4 + lax.rem(lax.rem(dev, 4) + z, 4),
    )


def opposite(step):
    x, core, y, z = step
    return (-x % 4, core, -y % 4, -z % 4)


BACK = [ORDER.index(opposite(step)) for step in ORDER] + [PEERS]


TURNS = [list(range(PEERS)), list(range(PEERS))[::-1]]


def across(row):
    return jnp.broadcast_to(row, (BLK, BLK))


def down(row):
    return jnp.broadcast_to(row, (BLK, BLK)).T


def column_sum(terms):
    return jnp.sum(terms, 0, keepdims=True)


def sort_rows(mine, names, lane):
    lane_row = lane[:1]
    key = mine * BLK + lane_row
    rank = column_sum(jnp.where(down(key) < across(key), 1.0, 0.0))
    at_rank = down(rank) == lane
    order = column_sum(jnp.where(at_rank, names, 0.0))
    mine_down = down(mine)
    sorted_mine = column_sum(jnp.where(at_rank, mine_down, 0.0))
    before = pltpu.roll(jnp.broadcast_to(sorted_mine, (8, BLK)), 1, 1)[:1]
    keep = jnp.where((sorted_mine == before) & (lane_row > 0), 1.0, 0.0)
    upto = column_sum(jnp.where(mine_down <= lane, 1.0, 0.0))
    has = column_sum(jnp.where(mine_down == lane, 1.0, 0.0))
    return [order, keep, jnp.maximum(upto - 1.0, 0.0), jnp.minimum(has, 1.0)]


def iotas():
    row = lax.broadcasted_iota(jnp.int32, (BLK, BLK), 0)
    lane = lax.broadcasted_iota(jnp.int32, (BLK, BLK), 1)
    return row, lane


def route(asked, owned, out):
    row, lane = iotas()
    lane_row = lane[:1]
    lane = lane.astype(jnp.float32)
    asked0, asked1, owned0, owned1 = asked[0:1], asked[1:2], owned[0:1], owned[1:2]
    owned_mine = owned1 & (BLOCKS - 1)
    first_near = jnp.where(asked0 >= 0, asked0 >> 5, BLOCKS)
    first_far = jnp.where(owned0 >= 0, owned0 & (BLOCKS - 1), BLOCKS)
    second = jnp.where(asked1 >= 0, asked1 >> 5, jnp.where(owned1 >= 0, owned_mine, BLOCKS))

    def shifted(values, lanes):
        return pltpu.roll(jnp.broadcast_to(values, (8, BLK)), lanes % BLK, 1)[:1]

    low = lane_row < PLACES
    paired = ((row % PLACES) * 2 + row // PLACES).astype(jnp.float32)
    single = row.astype(jnp.float32)
    for half in range(HALVES):
        shift = -half * PLACES
        both = jnp.where(low, shifted(first_near, shift), shifted(first_far, shift + PLACES))
        last = jnp.where(low, shifted(second, shift), BLOCKS)
        for table, mine, names in ((half, both, paired), (HALVES + half, last, single)):
            mine = mine.astype(jnp.float32)
            rows = sort_rows(mine, names, lane)
            rows += [jnp.minimum(mine, BLOCKS - 1.0), jnp.zeros((3, BLK), jnp.float32)]
            out[table * 8 : table * 8 + 8] = jnp.concatenate(rows, 0).astype(jnp.int32)
    asked_first = jnp.where(asked0 >= 0, asked0 >> 5, 0)
    asked_second = jnp.where(asked1 >= 0, asked1 >> 5, 0)
    both = (owned1 >= 0) & (asked1 >= 0)
    crowded = jnp.max(jnp.where(both, 1.0, 0.0), 1, keepdims=True)
    out[MISC : MISC + 8] = jnp.concatenate(
        [
            asked_first,
            asked_second,
            jnp.where(owned1 >= 0, owned_mine, asked_second),
            (asked1 >= 0).astype(jnp.int32),
            jnp.broadcast_to(crowded, (1, BLK)).astype(jnp.int32),
            jnp.zeros((3, BLK), jnp.int32),
        ],
        0,
    )


def route_rest(crowded, asked, owned, relay_shift, out):
    row, lane = iotas()
    lane = lane.astype(jnp.float32)
    lane_row = lane[:1]
    asked1, owned1 = asked[1:2], owned[1:2]
    ids = owned[2:3].astype(jnp.float32)
    rank = column_sum(jnp.where(down(ids) < across(ids), down(crowded), 0.0))
    rank_down = down(rank)
    hot_down = down(crowded) > 0.5
    my_rank = jnp.sum(jnp.where(lane_row == PEERS, rank, 0.0), 1, keepdims=True)
    count = jnp.sum(crowded, 1, keepdims=True)

    def pick(wanted, terms):
        wanted = jnp.where(wanted >= RANKS, wanted - RANKS, wanted)
        wanted = jnp.where(wanted < 0, wanted + RANKS, wanted)
        return column_sum(jnp.where(hot_down & (rank_down == across(wanted)), terms, 0.0))

    ahead = my_rank + lane_row
    behind = my_rank - lane_row
    asked_second = jnp.where(asked1 >= 0, asked1 >> 5, 0).astype(jnp.float32)
    both = (owned1 >= 0) & (asked1 >= 0)
    mine = jnp.where(both, owned1 & (BLOCKS - 1), BLOCKS).astype(jnp.float32)
    places = row.astype(jnp.float32)
    lend = pick(ahead, down(asked_second))
    source = pick(behind, places)
    found = pick(behind, jnp.ones((BLK, BLK), jnp.float32))
    mine = jnp.where((lane_row < RANKS) & (found > 0.5), pick(behind, down(mine)), float(BLOCKS))
    relay = pick(rank - relay_shift, places)
    rows = sort_rows(mine, places, lane)
    rows += [jnp.minimum(mine, BLOCKS - 1.0), lend, source, relay]
    out[...] = jnp.concatenate(rows, 0).astype(jnp.int32)
    return count


def with_norms(rows, extra):
    points, normals = rows[0:3], rows[3:6]
    square = points * points
    product = points * normals
    return jnp.concatenate(
        [
            rows[0:6],
            square[0:1] + square[1:2] + square[2:3] + extra,
            -(product[0:1] + product[1:2] + product[2:3]),
        ],
        0,
    )


def split(values):
    high = values.astype(jnp.bfloat16).astype(jnp.float32)
    rest = values - high
    middle = rest.astype(jnp.bfloat16).astype(jnp.float32)
    return high, middle, rest - middle


def other_features(rows):
    high, middle, low = split(with_norms(rows, softening))
    ones = jnp.where(lax.broadcasted_iota(jnp.int32, (8, BLK), 0) < 3, 1.0, 0.0)
    parts = [high, high, middle, middle, high, low, ones, jnp.zeros((8, BLK), jnp.float32)]
    return jnp.concatenate(parts, 0).T.astype(jnp.bfloat16)


def own_features(rows):
    pieces = split(with_norms(rows, 0.0))
    zero = jnp.zeros((1, BLK), jnp.float32)
    zeros3 = jnp.zeros((3, BLK), jnp.float32)
    columns = ([], [], [])
    for which in (0, 1, 0, 1, 2, 0):
        part = pieces[which]
        one = zero + 1.0 if which == 0 else zero
        columns[0].append(jnp.concatenate([part[3:6], zeros3, zero, zero], 0))
        columns[1].append(jnp.concatenate([zeros3, part[0:3], zero, one], 0))
        columns[2].append(jnp.concatenate([-2.0 * part[0:3], zeros3, one, zero], 0))
    tail = jnp.zeros((5, BLK), jnp.float32)
    blank = jnp.zeros((8, BLK), jnp.float32)
    for column, row in ((0, 7), (1, None), (2, 6)):
        if row is None:
            columns[column].append(blank)
        else:
            columns[column].append(
                jnp.concatenate([part[row : row + 1] for part in pieces] + [tail], 0)
            )
        columns[column].append(blank)
    return [jnp.concatenate(column, 0).astype(jnp.bfloat16) for column in columns]


def tile(rows, own):
    forms = jnp.dot(other_features(rows), own, preferred_element_type=jnp.float32)
    facing = jnp.maximum(forms[:, :BLK], 0.0) * jnp.maximum(forms[:, BLK : 2 * BLK], 0.0)
    distance_sq = forms[:, 2 * BLK :]
    bottom = math.pi * distance_sq * distance_sq
    inverse = pl.reciprocal(bottom, approx=True)
    inverse = inverse * (2.0 - bottom * inverse)
    return (facing * inverse).astype(jnp.bfloat16)


def fused_kernel(
    near_code,
    owned,
    emission,
    areas,
    material,
    reflect,
    positions,
    normals,
    out,
    fits,
    geometry,
    features,
    albedo,
    classes,
    scaled,
    total,
    running,
    send,
    last_send,
    near_send,
    near_recv,
    far_send,
    far_recv,
    asked_rows,
    table_rows,
    table,
    rest_rows,
    rest,
    tiles0,
    tiles1,
    last_tiles0,
    last_tiles1,
    recv00,
    recv01,
    recv10,
    recv11,
    last_recv00,
    last_recv01,
    last_recv10,
    last_recv11,
    lend_send,
    lend_recv0,
    lend_recv1,
    relay_send,
    relay_recv0,
    relay_recv1,
    rest_tiles,
    rest_values,
    send_sem,
    recv_sem,
    table_sem,
):
    tiles = (tiles0, tiles1)
    last_tiles = (last_tiles0, last_tiles1)
    recv = ((recv00, recv01), (recv10, recv11))
    last_recv = ((last_recv00, last_recv01), (last_recv10, last_recv11))
    lend_recv = (lend_recv0, lend_recv1)
    relay_recv = (relay_recv0, relay_recv1)
    grp, dev = lax.axis_index("grp"), lax.axis_index("dev")
    core = lax.rem(grp, 2)
    chip = (grp // 2) * 16 + dev
    peers = [peer(grp, dev, step) for step in ORDER]
    barrier = pltpu.get_barrier_semaphore()
    for other in peers:
        pl.semaphore_signal(barrier, inc=1, device_id=other, device_id_type=MESH)

    def describe(kind, source, target, halves=True):
        return [
            pltpu.make_async_remote_copy(
                src_ref=source(place),
                dst_ref=target(place),
                send_sem=send_sem.at[kind],
                recv_sem=recv_sem.at[kind * 2 + (place // PLACES if halves else 0)],
                device_id=other,
                device_id_type=MESH,
            )
            for place, other in enumerate(peers)
        ]

    def all_of(kind, ref, half=0):
        return pltpu.make_async_remote_copy(
            src_ref=ref,
            dst_ref=ref,
            send_sem=send_sem.at[kind],
            recv_sem=recv_sem.at[kind * 2 + half],
            device_id=peers[0],
            device_id_type=MESH,
        )

    def start(copies, first=0, count=PEERS):
        for turn in range(2):

            @pl.when(core == turn)
            def _():
                for place in TURNS[turn][first : first + count]:
                    copies[place].start()

    def exchange(kind, source, target, halves=True):
        start(describe(kind, source, target, halves))

    def came(kind, ref, half, each):
        count = (PLACES if half == 0 else PLACES - 1) * each
        all_of(kind, ref.at[pl.ds(0, count)], half).wait_recv()

    def left(kind, ref, count):
        all_of(kind, ref.at[pl.ds(0, count)]).wait_send()

    def firsts(sweep, first, count):
        def source(place):
            return send.at[pl.ds(place * 2 + first, count)]

        def target(place):
            half = recv[sweep][place // PLACES]
            return half.at[pl.ds(place % PLACES * 2 + first, count)]

        return source, target

    def lasts(sweep):
        def target(place):
            return last_recv[sweep][place // PLACES].at[place % PLACES]

        return lambda place: last_send.at[place], target

    def near_index(place, slot):
        return near_code[place * 2 + slot] & (BLOCKS - 1)

    def sent(row, place):
        return table[MISC + row, BACK[place]] & (BLOCKS - 1)

    def pack_near_values():
        def pack(place, _):
            send[place * 2] = scaled[near_index(place, 0)]
            return 0

        lax.fori_loop(0, DEVICES, pack, 0)

    def pack_far_values():
        for place in range(DEVICES):
            send[place * 2 + 1] = scaled[sent(0, place)]

    def pack_last_values(sweep):
        for place in range(DEVICES):
            last_send[place] = scaled[sent(2, place)]
        last_recv[sweep][1][PLACES - 1] = last_send[PEERS]

    def keep_own(sweep):
        for slot in range(2):
            recv[sweep][1][PLACES * 2 - 2 + slot] = send[PEERS * 2 + slot]

    sides = [[place for place in range(PEERS) if ORDER[place][1] == side] for side in range(2)]

    def on_core(side, act):
        @pl.when(core == side)
        def _():
            act()

    def lend(sweep):
        for apart in range(RANKS):
            block = scaled[rest[5, apart] & (BLOCKS - 1)]
            for piece in range(PIECES):
                lend_send[apart * PIECES + piece] = block[piece * ROWS : (piece + 1) * ROWS]
        lend_recv[sweep][PEERS] = lend_send[chip]
        copies = describe(
            7 + sweep,
            lambda place: lend_send.at[(peers[place][0] // 2) * 16 + peers[place][1]],
            lambda place: lend_recv[sweep].at[place],
            False,
        )
        for side in range(2):
            on_core(side, lambda: [copies[place].start() for place in sides[side]] and None)

    def pass_on(sweep):
        copies = describe(
            9 + sweep,
            lambda place: relay_send.at[place],
            lambda place: relay_recv[sweep].at[chip],
            False,
        )

        @pl.when(core == 0)
        def _():
            all_of(7 + sweep, lend_recv[sweep].at[pl.ds(0, PEERS)]).wait_recv()
            for place in range(DEVICES):
                relay_send[place] = lend_recv[sweep][rest[7, BACK[place]] & (DEVICES - 1)]
            relay_recv[sweep][chip] = relay_send[PEERS]
            for place in range(PEERS):
                copies[place].start()

    def passed_came(sweep):
        for side in range(2):
            pieces = relay_recv[sweep].at[pl.ds(0, len(sides[side]))]
            on_core(side, lambda: all_of(9 + sweep, pieces).wait_recv())

    def rest_left(sweep):
        for side in range(2):
            on_core(side, lambda: left(7 + sweep, lend_send, len(sides[side])))
        on_core(0, lambda: left(9 + sweep, relay_send, PEERS))

    for block in range(BLOCKS):
        lanes = pl.ds(block * BLK, BLK)
        geometry[block] = jnp.concatenate(
            [positions[:, lanes], normals[:, lanes], jnp.zeros((2, BLK), jnp.float32)], 0
        )
    lane = lax.broadcasted_iota(jnp.int32, (4, BLK), 1)

    def pack_near(place, _):
        first, second = near_code[place * 2], near_code[place * 2 + 1]
        codes = jnp.where(lane == 0, first, jnp.where(lane == 1, second, 0)).astype(jnp.float32)
        rows = [geometry[near_index(place, slot)][:6] for slot in range(2)]
        near_send[place] = jnp.concatenate(rows + [codes], 0)
        return 0

    lax.fori_loop(0, DEVICES, pack_near, 0)
    near_recv[PEERS] = near_send[PEERS]
    for block in range(BLOCKS):
        lanes = pl.ds(block * BLK, BLK)
        scaled[block] = (emission[:, lanes] * areas[:, lanes]).astype(jnp.bfloat16)
    pl.semaphore_wait(barrier, PEERS)
    exchange(0, lambda place: near_send.at[place], lambda place: near_recv.at[place], False)
    pack_near_values()
    exchange(2, *firsts(0, 0, 1))

    for which in range(classes.shape[0]):
        classes[which] = jnp.broadcast_to(reflect[:, which : which + 1], (BANDS, BLK))
    for block in range(BLOCKS):
        lanes = pl.ds(block * BLK, BLK)
        row = material[:, lanes]
        part = classes[0]
        for which in range(1, classes.shape[0]):
            part = jnp.where(row == which, classes[which], part)
        albedo[:, lanes] = part

    def build_features(block, _):
        for index, column in enumerate(own_features(geometry[block])):
            features[block, :, index * BLK : (index + 1) * BLK] = column
        return 0

    lax.fori_loop(0, BLOCKS, build_features, 0)

    all_of(0, near_recv.at[pl.ds(0, PEERS)]).wait_recv()

    def collect_asked(place, _):
        asked_rows[pl.ds(place, 1)] = near_recv[place, 12:13]
        return 0

    lax.fori_loop(0, DEVICES, collect_asked, 0)
    asked = asked_rows[...].T[:8].astype(jnp.int32)
    route(asked, owned[...], table_rows)
    to_table = pltpu.make_async_copy(table_rows, table, table_sem.at[0])
    to_table.start()
    to_table.wait()

    crowded_row = table_rows[MISC + 4 : MISC + 5].astype(jnp.float32)
    blank = jnp.zeros((3, BLK), jnp.float32)
    for place in range(DEVICES):
        rows = [geometry[sent(slot, place)][:6] for slot in range(2)]
        far_send[place] = jnp.concatenate(rows + [crowded_row, blank], 0)
    far_recv[PEERS] = far_send[PEERS]
    exchange(1, lambda place: far_send.at[place], lambda place: far_recv.at[place], False)
    pack_far_values()
    keep_own(0)
    exchange(3, *firsts(0, 1, 1))
    pack_last_values(0)
    last_copies = describe(4, *lasts(0))
    start(last_copies, 0, PLACES)

    def own_side(group, task):
        return features[table[group * 8 + 4, task] & (BLOCKS - 1)]

    def build(source, slot, half):
        def step(pair, _):
            for inner in range(2):
                place = pair * 2 + inner
                rows = source[half * PLACES + place][:6]
                tiles[half][place * 2 + slot] = tile(rows, own_side(half, slot * PLACES + place))
            return 0

        lax.fori_loop(0, PLACES // 2, step, 0)

    for half in range(HALVES):
        build(near_recv, 0, half)

    all_of(1, far_recv.at[pl.ds(0, PEERS)]).wait_recv()

    def collect_crowded(place, _):
        asked_rows[pl.ds(place, 1)] = far_recv[place, 12:13]
        return 0

    lax.fori_loop(0, DEVICES, collect_crowded, 0)
    crowded = asked_rows[...].T[:1]
    shift = (chip // PIECES).astype(jnp.float32)
    count = route_rest(crowded, asked, owned[...], shift, rest_rows)
    fits[...] = jnp.broadcast_to(count, (8, BLK))
    to_rest = pltpu.make_async_copy(rest_rows, rest, table_sem.at[1])
    to_rest.start()
    to_rest.wait()
    lend(0)
    start(last_copies, PLACES, PEERS - PLACES)

    for half in range(HALVES):
        build(far_recv, 1, half)
    pass_on(0)

    for half in range(HALVES):

        def build_last(pair, _):
            for inner in range(2):
                place = pair * 2 + inner
                whole = half * PLACES + place
                near = table[MISC + 3, whole] > 0
                rows = jnp.where(near, near_recv[whole], far_recv[whole])[6:12]
                last_tiles[half][place] = tile(rows, own_side(HALVES + half, place))
            return 0

        lax.fori_loop(0, PLACES // 2, build_last, 0)

    def build_rest(apart, _):
        rows = far_recv[rest[6, apart] & (DEVICES - 1)][6:12]
        rest_tiles[apart] = tile(rows, features[rest[4, apart] & (BLOCKS - 1)])
        return 0

    lax.fori_loop(0, RANKS, build_rest, 0)

    def accumulate(values_ref, tiles_ref, rows, base, first):
        tasks = values_ref.shape[0]

        def add(group, run):
            for inner in range(8):
                task = group * 8 + inner
                index = rows[base, task] & (tasks - 1)
                run = run * rows[base + 1, task].astype(jnp.float32) + jnp.dot(
                    values_ref[index], tiles_ref[index], preferred_element_type=jnp.float32
                )
                running[task] = run
            return run

        lax.fori_loop(0, tasks // 8, add, jnp.zeros((BANDS, BLK), jnp.float32))

        def fold(block, _):
            part = running[rows[base + 2, block] & (tasks - 1)]
            part = part * rows[base + 3, block].astype(jnp.float32)
            total[block] = part if first else total[block] + part
            return 0

        lax.fori_loop(0, BLOCKS, fold, 0)

    for sweep in range(SWEEPS):
        if sweep == 0:
            rounds = ((2, 1), (3, 1))
        else:
            rounds = ((5, 2),)
            lend(1)
            pack_near_values()
            pack_far_values()
            exchange(5, *firsts(1, 0, 2))
            keep_own(1)
            pack_last_values(1)
            pass_on(1)
            exchange(6, *lasts(1))

        for half in range(HALVES):
            for kind, each in rounds:
                came(kind, recv[sweep][half], half, each)
            accumulate(recv[sweep][half], tiles[half], table, half * 8, half == 0)
        for kind, each in rounds:
            left(kind, send, PEERS * each)

        passed_came(sweep)
        for apart in range(RANKS):
            for piece in range(PIECES):
                rest_values[apart, piece * ROWS : (piece + 1) * ROWS] = relay_recv[sweep][
                    apart * PIECES + piece
                ]
        accumulate(rest_values, rest_tiles, rest, 0, False)
        rest_left(sweep)
        if sweep == 0:
            left(0, near_send, PEERS)
            left(1, far_send, PEERS)

        for half in range(HALVES):
            came(4 + 2 * sweep, last_recv[sweep][half], half, 1)
            accumulate(
                last_recv[sweep][half], last_tiles[half], table, (HALVES + half) * 8, False
            )
        left(4 + 2 * sweep, last_send, PEERS)

        for block in range(BLOCKS):
            lanes = pl.ds(block * BLK, BLK)
            reflected = albedo[:, lanes] * total[block]
            if sweep + 1 < SWEEPS:
                current = emission[:, lanes] + reflected
                scaled[block] = (current * areas[:, lanes]).astype(jnp.bfloat16)
            else:
                out[:, lanes] = reflected


def fused(near_code, owned, emission, areas, material, reflect, positions, normals):
    smem = pl.BlockSpec(memory_space=pltpu.SMEM)
    vmem = pl.BlockSpec(memory_space=pltpu.VMEM)
    values = pltpu.VMEM((PLACES * 2, BANDS, BLK), jnp.bfloat16)
    last_values = pltpu.VMEM((PLACES, BANDS, BLK), jnp.bfloat16)
    tiles = pltpu.VMEM((PLACES * 2, BLK, BLK), jnp.bfloat16)
    last_tiles = pltpu.VMEM((PLACES, BLK, BLK), jnp.bfloat16)
    message = pltpu.VMEM((DEVICES, 16, BLK), jnp.float32)
    lent = pltpu.VMEM((DEVICES, ROWS, BLK), jnp.bfloat16)
    passed = pltpu.VMEM((RELAYS, ROWS, BLK), jnp.bfloat16)
    return pl.pallas_call(
        fused_kernel,
        in_specs=[smem] + [vmem] * 7,
        out_specs=[vmem, vmem],
        out_shape=[
            jax.ShapeDtypeStruct(emission.shape, jnp.float32),
            jax.ShapeDtypeStruct((8, BLK), jnp.float32),
        ],
        scratch_shapes=[
            pltpu.VMEM((BLOCKS, 8, BLK), jnp.float32),
            pltpu.VMEM((BLOCKS, FEATURES, 3 * BLK), jnp.bfloat16),
            pltpu.VMEM(emission.shape, jnp.float32),
            pltpu.VMEM((reflect.shape[1], BANDS, BLK), jnp.float32),
            pltpu.VMEM((BLOCKS, BANDS, BLK), jnp.bfloat16),
            pltpu.VMEM((BLOCKS, BANDS, BLK), jnp.float32),
            pltpu.VMEM((PLACES * 2, BANDS, BLK), jnp.float32),
            pltpu.VMEM((DEVICES * 2, BANDS, BLK), jnp.bfloat16),
            pltpu.VMEM((DEVICES, BANDS, BLK), jnp.bfloat16),
            message,
            message,
            message,
            message,
            pltpu.VMEM((DEVICES, BLK), jnp.float32),
            pltpu.VMEM((MISC + 8, BLK), jnp.int32),
            pltpu.SMEM((MISC + 8, BLK), jnp.int32),
            pltpu.VMEM((8, BLK), jnp.int32),
            pltpu.SMEM((8, BLK), jnp.int32),
        ]
        + [tiles] * HALVES
        + [last_tiles] * HALVES
        + [values] * (SWEEPS * HALVES)
        + [last_values] * (SWEEPS * HALVES)
        + [passed, lent, lent, lent, passed, passed]
        + [
            pltpu.VMEM((RANKS, BLK, BLK), jnp.bfloat16),
            pltpu.VMEM((RANKS, BANDS, BLK), jnp.bfloat16),
            pltpu.SemaphoreType.DMA((11,)),
            pltpu.SemaphoreType.DMA((22,)),
            pltpu.SemaphoreType.DMA((2,)),
        ],
        compiler_params=pltpu.CompilerParams(
            collective_id=0, has_side_effects=True, vmem_limit_bytes=62 << 20
        ),
        name="fused",
    )(near_code, owned, emission, areas, material, reflect, positions, normals)


def on_device(
    emission, positions, normals, areas, material, reflect, pair_local, pair_device, pair_block
):
    grp, dev = lax.axis_index("grp"), lax.axis_index("dev")
    pairs = pair_local.shape[0]

    steps = np.array(ORDER + [(0, 0, 0, 0)], np.int32).T
    there = peer(grp, dev, steps)
    there = there[0] * 16 + there[1]
    here = peer(grp, dev, (-steps) % np.array([[4], [2], [4], [4]], np.int32))
    here = here[0] * 16 + here[1]
    target = pair_device[:, 0]
    pair_order = jnp.arange(pairs, dtype=jnp.int32)
    earlier = (target[:, None] == target[None, :]) & (pair_order[None, :] < pair_order[:, None])
    second = jnp.any(earlier, 1)
    code = pair_block * BLOCKS + pair_local

    def named(ids, is_second):
        found = (target[None, :] == ids[:, None]) & (second == is_second)[None, :]
        return jnp.max(jnp.where(found, code[None, :], -1), 1)

    near_code = jnp.stack([named(there, False), named(there, True)], 1).reshape(-1)
    owned = jnp.stack([named(here, False), named(here, True), here] + [here * 0] * 5, 0)

    reflected, crowded = fused(
        near_code,
        owned,
        emission,
        areas[None, :],
        material[None, :],
        reflect,
        positions,
        normals,
    )
    return lax.cond(
        crowded[0, 0] <= RANKS,
        lambda: emission + reflected,
        lambda: general(
            emission,
            positions,
            normals,
            areas,
            material,
            reflect,
            pair_local,
            pair_device,
            pair_block,
        ),
    )


def solution(mesh):
    return jax.shard_map(
        on_device,
        mesh=mesh,
        in_specs=(
            P(None, AXES),
            P(None, AXES),
            P(None, AXES),
            P(AXES),
            P(AXES),
            P(),
            P(AXES),
            P(AXES, None),
            P(AXES),
        ),
        out_specs=P(None, AXES),
        check_vma=False,
    )
```

profile of v0, /device:TPU:1, one launch (start us, length us, event | category | flops | bytes accessed | tf_op | source)
XLA Modules:
  0.0 213.3 jit_solution(2005232249195995439)
XLA Ops:
  0.0 0.8 fusion.81
  0.8 0.9 fusion.73
  1.7 0.9 select_reduce_fusion.1
  2.6 0.1 copy.49
  2.7 0.7 reshape.70.near_code
  3.5 0.6 stack.35.owned
  4.1 1.4 copy.50.reflect
  5.5 203.0 %fused.1 = (f32[64,4096]{1,0:T(8,128)}, f32[8,128]{1,0:T(8,128)}) custom-call(s32[256]{0:T(256)} %reshape.70.near_code, s32[8,128]{1,0:T(8,128)} %stack.35.owned, f32[64,4096]{1,0:T(8,128)} %emission.1, f32[1,4096]{1,0:T(1,128)} %bitcast.90, s32[1,4096]{1,0:T(1,128)} %bitcast.89, f32[64,16]{1,0:T(8,128)} %copy.50.reflect, f32[3,4096]{1,0:T(4,128)} %positions.1, ...), custom_call_target="tpu_custom_call" | custom-call | tf_op jit(solution)/shard_map/fused/pallas_call | solution.py:722
  208.5 1.2 slice.54
  210.4 1.9 conditional.1
  210.6 1.7 add.113
  212.3 0.0 copy-start
  212.3 1.0 copy-done
  (4 shorter events, 0.0 us)
Async XLA Ops:
  212.3 1.0 copy-start
where the time goes:
time: 214 us; the launch traced here: 213 us
  Pallas kernels  203 us (95%)
  local copies, waits for them, and re-layouts  5.01 us (2%)
  other arithmetic  4.24 us (2%)
    pallas_call x1, Pallas kernels, fused(): pl.pallas_call(fused_kernel, in_specs=[smem] + [vmem] * 7, out_specs=[vme...  203 us

commit v1 on v0

--- a/solution.py
+++ b/solution.py
@@ -138,7 +138,7 @@
 BACK = [ORDER.index(opposite(step)) for step in ORDER] + [PEERS]
 
 
-TURNS = [list(range(PEERS)), list(range(PEERS))[::-1]]
+TURNS = [list(range(PEERS)), [ORDER.index((y, core, z, x)) for x, core, y, z in ORDER]]
 
 
 def across(row):
@@ -172,6 +172,30 @@
     row = lax.broadcasted_iota(jnp.int32, (BLK, BLK), 0)
     lane = lax.broadcasted_iota(jnp.int32, (BLK, BLK), 1)
     return row, lane
+
+
+def name_rows(grp, dev, steps, target, code):
+    row, lane = iotas()
+
+    def ids(first):
+        x, core, y, z = (steps[first + part : first + part + 1] for part in range(4))
+        x, core = (x + grp // 2) & 3, (core + lax.rem(grp, 2)) & 1
+        y, z = (y + dev // 4) & 3, (z + lax.rem(dev, 4)) & 3
+        return ((x * 2 + core) * 16 + y * 4 + z).astype(jnp.float32)
+
+    there, here = ids(0), ids(4)
+    target, code = target.astype(jnp.float32), code.astype(jnp.float32)
+    target_down, code_down = down(target), down(code)
+    earlier = (target_down == across(target)) & (row < lane)
+    second = jnp.max(jnp.where(earlier, 1.0, 0.0), 0, keepdims=True)
+    second_down = down(second)
+
+    def named(ids, which):
+        found = (target_down == across(ids)) & (second_down == which)
+        return jnp.max(jnp.where(found, code_down, -1.0), 0, keepdims=True)
+
+    rows = [named(there, 0.0), named(there, 1.0), named(here, 0.0), named(here, 1.0), here]
+    return jnp.concatenate(rows + [jnp.zeros((3, BLK), jnp.float32)], 0).astype(jnp.int32)
 
 
 def route(asked, owned, out):
@@ -245,9 +269,9 @@
     mine = jnp.where((lane_row < RANKS) & (found > 0.5), pick(behind, down(mine)), float(BLOCKS))
     relay = pick(rank - relay_shift, places)
     rows = sort_rows(mine, places, lane)
+    lend = jnp.where(lane_row == BLK - 1, count, lend)
     rows += [jnp.minimum(mine, BLOCKS - 1.0), lend, source, relay]
     out[...] = jnp.concatenate(rows, 0).astype(jnp.int32)
-    return count
 
 
 def with_norms(rows, extra):
@@ -313,8 +337,10 @@
 
 
 def fused_kernel(
-    near_code,
-    owned,
+    steps,
+    target,
+    pair_block,
+    pair_local,
     emission,
     areas,
     material,
@@ -323,6 +349,8 @@
     normals,
     out,
     fits,
+    name_table,
+    names,
     geometry,
     features,
     albedo,
@@ -437,7 +465,7 @@
         return lambda place: last_send.at[place], target
 
     def near_index(place, slot):
-        return near_code[place * 2 + slot] & (BLOCKS - 1)
+        return names[slot, place] & (BLOCKS - 1)
 
     def sent(row, place):
         return table[MISC + row, BACK[place]] & (BLOCKS - 1)
@@ -511,15 +539,21 @@
             on_core(side, lambda: left(7 + sweep, lend_send, len(sides[side])))
         on_core(0, lambda: left(9 + sweep, relay_send, PEERS))
 
+    code = pair_block[...] * BLOCKS + pair_local[...]
+    name_table[...] = name_rows(grp, dev, steps[...], target[...], code)
+    to_names = pltpu.make_async_copy(name_table, names, table_sem.at[2])
+    to_names.start()
+
     for block in range(BLOCKS):
         lanes = pl.ds(block * BLK, BLK)
         geometry[block] = jnp.concatenate(
             [positions[:, lanes], normals[:, lanes], jnp.zeros((2, BLK), jnp.float32)], 0
         )
+    to_names.wait()
     lane = lax.broadcasted_iota(jnp.int32, (4, BLK), 1)
 
     def pack_near(place, _):
-        first, second = near_code[place * 2], near_code[place * 2 + 1]
+        first, second = names[0, place], names[1, place]
         codes = jnp.where(lane == 0, first, jnp.where(lane == 1, second, 0)).astype(jnp.float32)
         rows = [geometry[near_index(place, slot)][:6] for slot in range(2)]
         near_send[place] = jnp.concatenate(rows + [codes], 0)
@@ -535,8 +569,9 @@
     pack_near_values()
     exchange(2, *firsts(0, 0, 1))
 
+    by_band = jnp.concatenate([reflect[...], jnp.zeros_like(reflect[...])], 1).T[:BANDS]
     for which in range(classes.shape[0]):
-        classes[which] = jnp.broadcast_to(reflect[:, which : which + 1], (BANDS, BLK))
+        classes[which] = jnp.broadcast_to(by_band[:, which : which + 1], (BANDS, BLK))
     for block in range(BLOCKS):
         lanes = pl.ds(block * BLK, BLK)
         row = material[:, lanes]
@@ -560,7 +595,7 @@
 
     lax.fori_loop(0, DEVICES, collect_asked, 0)
     asked = asked_rows[...].T[:8].astype(jnp.int32)
-    route(asked, owned[...], table_rows)
+    route(asked, name_table[2:5], table_rows)
     to_table = pltpu.make_async_copy(table_rows, table, table_sem.at[0])
     to_table.start()
     to_table.wait()
@@ -604,11 +639,11 @@
     lax.fori_loop(0, DEVICES, collect_crowded, 0)
     crowded = asked_rows[...].T[:1]
     shift = (chip // PIECES).astype(jnp.float32)
-    count = route_rest(crowded, asked, owned[...], shift, rest_rows)
-    fits[...] = jnp.broadcast_to(count, (8, BLK))
+    route_rest(crowded, asked, name_table[2:5], shift, rest_rows)
     to_rest = pltpu.make_async_copy(rest_rows, rest, table_sem.at[1])
     to_rest.start()
     to_rest.wait()
+    fits[0, 0] = rest[5, BLK - 1]
     lend(0)
     start(last_copies, PLACES, PEERS - PLACES)
 
@@ -709,7 +744,7 @@
                 out[:, lanes] = reflected
 
 
-def fused(near_code, owned, emission, areas, material, reflect, positions, normals):
+def fused(steps, target, pair_block, pair_local, emission, areas, material, reflect, positions, normals):
     smem = pl.BlockSpec(memory_space=pltpu.SMEM)
     vmem = pl.BlockSpec(memory_space=pltpu.VMEM)
     values = pltpu.VMEM((PLACES * 2, BANDS, BLK), jnp.bfloat16)
@@ -721,17 +756,19 @@
     passed = pltpu.VMEM((RELAYS, ROWS, BLK), jnp.bfloat16)
     return pl.pallas_call(
         fused_kernel,
-        in_specs=[smem] + [vmem] * 7,
-        out_specs=[vmem, vmem],
+        in_specs=[vmem] * 10,
+        out_specs=[vmem, smem],
         out_shape=[
             jax.ShapeDtypeStruct(emission.shape, jnp.float32),
-            jax.ShapeDtypeStruct((8, BLK), jnp.float32),
+            jax.ShapeDtypeStruct((1, 1), jnp.int32),
         ],
         scratch_shapes=[
+            pltpu.VMEM((8, BLK), jnp.int32),
+            pltpu.SMEM((8, BLK), jnp.int32),
             pltpu.VMEM((BLOCKS, 8, BLK), jnp.float32),
             pltpu.VMEM((BLOCKS, FEATURES, 3 * BLK), jnp.bfloat16),
             pltpu.VMEM(emission.shape, jnp.float32),
-            pltpu.VMEM((reflect.shape[1], BANDS, BLK), jnp.float32),
+            pltpu.VMEM((reflect.shape[0], BANDS, BLK), jnp.float32),
             pltpu.VMEM((BLOCKS, BANDS, BLK), jnp.bfloat16),
             pltpu.VMEM((BLOCKS, BANDS, BLK), jnp.float32),
             pltpu.VMEM((PLACES * 2, BANDS, BLK), jnp.float32),
@@ -757,46 +794,40 @@
             pltpu.VMEM((RANKS, BANDS, BLK), jnp.bfloat16),
             pltpu.SemaphoreType.DMA((11,)),
             pltpu.SemaphoreType.DMA((22,)),
-            pltpu.SemaphoreType.DMA((2,)),
+            pltpu.SemaphoreType.DMA((3,)),
         ],
         compiler_params=pltpu.CompilerParams(
             collective_id=0, has_side_effects=True, vmem_limit_bytes=62 << 20
         ),
         name="fused",
-    )(near_code, owned, emission, areas, material, reflect, positions, normals)
+    )(
+        steps,
+        target,
+        pair_block,
+        pair_local,
+        emission,
+        areas,
+        material,
+        reflect,
+        positions,
+        normals,
+    )
 
 
 def on_device(
     emission, positions, normals, areas, material, reflect, pair_local, pair_device, pair_block
 ):
-    grp, dev = lax.axis_index("grp"), lax.axis_index("dev")
-    pairs = pair_local.shape[0]
-
-    steps = np.array(ORDER + [(0, 0, 0, 0)], np.int32).T
-    there = peer(grp, dev, steps)
-    there = there[0] * 16 + there[1]
-    here = peer(grp, dev, (-steps) % np.array([[4], [2], [4], [4]], np.int32))
-    here = here[0] * 16 + here[1]
-    target = pair_device[:, 0]
-    pair_order = jnp.arange(pairs, dtype=jnp.int32)
-    earlier = (target[:, None] == target[None, :]) & (pair_order[None, :] < pair_order[:, None])
-    second = jnp.any(earlier, 1)
-    code = pair_block * BLOCKS + pair_local
-
-    def named(ids, is_second):
-        found = (target[None, :] == ids[:, None]) & (second == is_second)[None, :]
-        return jnp.max(jnp.where(found, code[None, :], -1), 1)
-
-    near_code = jnp.stack([named(there, False), named(there, True)], 1).reshape(-1)
-    owned = jnp.stack([named(here, False), named(here, True), here] + [here * 0] * 5, 0)
-
+    steps = ORDER + [(0, 0, 0, 0)]
+    steps = np.array([step + opposite(step) for step in steps], np.int32).T
     reflected, crowded = fused(
-        near_code,
-        owned,
+        jnp.asarray(steps),
+        pair_device.reshape(1, -1),
+        pair_block[None, :],
+        pair_local[None, :],
         emission,
         areas[None, :],
         material[None, :],
-        reflect,
+        reflect.T,
         positions,
         normals,
     )

time: 214 us -> 205 us (0.958)
  local copies, waits for them, and re-layouts: 5.01 us -> 0.96 us
  other arithmetic: 4.24 us -> 1.65 us
where the time goes in v1:
time: 205 us
  Pallas kernels  202 us (99%)
    pallas_call x1, Pallas kernels, fused(): pl.pallas_call(fused_kernel, in_specs=[vmem] * 10, out_specs=[vmem, smem]...  202 us

profile of v1, /device:TPU:1, one launch (start us, length us, event | category | flops | bytes accessed | tf_op | source)
XLA Modules:
  0.0 205.3 jit_solution(11826379642126096612)
XLA Ops:
  0.0 201.9 %fused.1 = (f32[64,4096]{1,0:T(8,128)}, s32[1,1]{1,0:T(1,128)}) custom-call(s32[8,128]{1,0:T(8,128)} %constant.8.clone.steps, s32[1,128]{1,0:T(1,128)} %bitcast.139, s32[1,128]{1,0:T(1,128)} %bitcast.144, s32[1,128]{1,0:T(1,128)} %bitcast.142, f32[64,4096]{1,0:T(8,128)} %emission.1, f32[1,4096]{1,0:T(1,128)} %bitcast.88, s32[1,4096]{1,0:T(1,128)} %bitcast.87, ...), custom_call_target="tpu_custom_call" | custom-call | tf_op jit(solution)/shard_map/fused/pallas_call | solution.py:757
  202.4 1.9 conditional.1
  202.7 1.7 add.69
  204.3 0.0 copy-start
  204.4 1.0 copy-done
Async XLA Ops:
  204.3 1.0 copy-start

commit v2 on v1

--- a/solution.py
+++ b/solution.py
@@ -230,9 +230,9 @@
     out[MISC : MISC + 8] = jnp.concatenate(
         [
             asked_first,
-            asked_second,
+            jnp.zeros((1, BLK), jnp.int32),
             jnp.where(owned1 >= 0, owned_mine, asked_second),
-            (asked1 >= 0).astype(jnp.int32),
+            jnp.zeros((1, BLK), jnp.int32),
             jnp.broadcast_to(crowded, (1, BLK)).astype(jnp.int32),
             jnp.zeros((3, BLK), jnp.int32),
         ],
@@ -387,6 +387,10 @@
     relay_send,
     relay_recv0,
     relay_recv1,
+    shape_send,
+    shape_recv,
+    shape_relay,
+    shape_came,
     rest_tiles,
     rest_values,
     send_sem,
@@ -404,7 +408,7 @@
     chip = (grp // 2) * 16 + dev
     peers = [peer(grp, dev, step) for step in ORDER]
     barrier = pltpu.get_barrier_semaphore()
-    for other in peers:
+    for other in peers[::-1]:
         pl.semaphore_signal(barrier, inc=1, device_id=other, device_id_type=MESH)
 
     def describe(kind, source, target, halves=True):
@@ -464,6 +468,14 @@
 
         return lambda place: last_send.at[place], target
 
+    def at_places(act):
+        def step(group, _):
+            for inner in range(8):
+                act(group * 8 + inner)
+            return 0
+
+        lax.fori_loop(0, DEVICES // 8, step, 0)
+
     def near_index(place, slot):
         return names[slot, place] & (BLOCKS - 1)
 
@@ -471,11 +483,10 @@
         return table[MISC + row, BACK[place]] & (BLOCKS - 1)
 
     def pack_near_values():
-        def pack(place, _):
+        def pack(place):
             send[place * 2] = scaled[near_index(place, 0)]
-            return 0
-
-        lax.fori_loop(0, DEVICES, pack, 0)
+
+        at_places(pack)
 
     def pack_far_values():
         for place in range(DEVICES):
@@ -529,6 +540,58 @@
             for place in range(PEERS):
                 copies[place].start()
 
+    z = lax.rem(dev, 4)
+    is_relay = (core == 0) & (z == 0)
+    not_relay = jnp.logical_not(is_relay)
+
+    def lend_geometry():
+        for apart in range(RANKS):
+            shape_send[apart] = geometry[rest[5, apart] & (BLOCKS - 1)]
+        shape_recv[PEERS] = shape_send[chip // PIECES]
+        copies = describe(
+            11,
+            lambda place: shape_send.at[(peers[place][0] // 2) * 4 + peers[place][1] // 4],
+            lambda place: shape_recv.at[place],
+            False,
+        )
+        for side in range(2):
+            for level in range(4):
+
+                @pl.when((core == side) & (z == level))
+                def _():
+                    for place in sides[side]:
+                        if (level + ORDER[place][3]) % 4 == 0:
+                            copies[place].start()
+
+    def pass_geometry_on():
+        copies = describe(
+            12,
+            lambda place: shape_relay.at[place],
+            lambda place: shape_came.at[chip // PIECES],
+            False,
+        )
+
+        @pl.when(is_relay)
+        def _():
+            all_of(11, shape_recv.at[pl.ds(0, PEERS)]).wait_recv()
+            for place in range(DEVICES):
+                shape_relay[place] = shape_recv[rest[7, BACK[place]] & (DEVICES - 1)]
+            shape_came[chip // PIECES] = shape_relay[PEERS]
+            for place in range(PEERS):
+                copies[place].start()
+
+    def geometry_came():
+        for condition, count in ((is_relay, RANKS - 1), (not_relay, RANKS)):
+
+            @pl.when(condition)
+            def _():
+                all_of(12, shape_came.at[pl.ds(0, count)]).wait_recv()
+                left(11, shape_send, count)
+
+        @pl.when(is_relay)
+        def _():
+            left(12, shape_relay, PEERS)
+
     def passed_came(sweep):
         for side in range(2):
             pieces = relay_recv[sweep].at[pl.ds(0, len(sides[side]))]
@@ -550,22 +613,20 @@
             [positions[:, lanes], normals[:, lanes], jnp.zeros((2, BLK), jnp.float32)], 0
         )
     to_names.wait()
-    lane = lax.broadcasted_iota(jnp.int32, (4, BLK), 1)
-
-    def pack_near(place, _):
+    lane = lax.broadcasted_iota(jnp.int32, (2, BLK), 1)
+
+    def pack_near(place):
         first, second = names[0, place], names[1, place]
         codes = jnp.where(lane == 0, first, jnp.where(lane == 1, second, 0)).astype(jnp.float32)
-        rows = [geometry[near_index(place, slot)][:6] for slot in range(2)]
-        near_send[place] = jnp.concatenate(rows + [codes], 0)
-        return 0
-
-    lax.fori_loop(0, DEVICES, pack_near, 0)
+        near_send[place] = jnp.concatenate([geometry[near_index(place, 0)][:6], codes], 0)
+
+    at_places(pack_near)
     near_recv[PEERS] = near_send[PEERS]
+    pl.semaphore_wait(barrier, PEERS)
+    exchange(0, lambda place: near_send.at[place], lambda place: near_recv.at[place], False)
     for block in range(BLOCKS):
         lanes = pl.ds(block * BLK, BLK)
         scaled[block] = (emission[:, lanes] * areas[:, lanes]).astype(jnp.bfloat16)
-    pl.semaphore_wait(barrier, PEERS)
-    exchange(0, lambda place: near_send.at[place], lambda place: near_recv.at[place], False)
     pack_near_values()
     exchange(2, *firsts(0, 0, 1))
 
@@ -589,11 +650,10 @@
 
     all_of(0, near_recv.at[pl.ds(0, PEERS)]).wait_recv()
 
-    def collect_asked(place, _):
-        asked_rows[pl.ds(place, 1)] = near_recv[place, 12:13]
-        return 0
-
-    lax.fori_loop(0, DEVICES, collect_asked, 0)
+    def collect_asked(place):
+        asked_rows[pl.ds(place, 1)] = near_recv[place, 6:7]
+
+    at_places(collect_asked)
     asked = asked_rows[...].T[:8].astype(jnp.int32)
     route(asked, name_table[2:5], table_rows)
     to_table = pltpu.make_async_copy(table_rows, table, table_sem.at[0])
@@ -603,7 +663,7 @@
     crowded_row = table_rows[MISC + 4 : MISC + 5].astype(jnp.float32)
     blank = jnp.zeros((3, BLK), jnp.float32)
     for place in range(DEVICES):
-        rows = [geometry[sent(slot, place)][:6] for slot in range(2)]
+        rows = [geometry[sent(row, place)][:6] for row in (0, 2)]
         far_send[place] = jnp.concatenate(rows + [crowded_row, blank], 0)
     far_recv[PEERS] = far_send[PEERS]
     exchange(1, lambda place: far_send.at[place], lambda place: far_recv.at[place], False)
@@ -632,11 +692,10 @@
 
     all_of(1, far_recv.at[pl.ds(0, PEERS)]).wait_recv()
 
-    def collect_crowded(place, _):
+    def collect_crowded(place):
         asked_rows[pl.ds(place, 1)] = far_recv[place, 12:13]
-        return 0
-
-    lax.fori_loop(0, DEVICES, collect_crowded, 0)
+
+    at_places(collect_crowded)
     crowded = asked_rows[...].T[:1]
     shift = (chip // PIECES).astype(jnp.float32)
     route_rest(crowded, asked, name_table[2:5], shift, rest_rows)
@@ -644,11 +703,13 @@
     to_rest.start()
     to_rest.wait()
     fits[0, 0] = rest[5, BLK - 1]
+    lend_geometry()
     lend(0)
     start(last_copies, PLACES, PEERS - PLACES)
 
     for half in range(HALVES):
         build(far_recv, 1, half)
+    pass_geometry_on()
     pass_on(0)
 
     for half in range(HALVES):
@@ -656,20 +717,16 @@
         def build_last(pair, _):
             for inner in range(2):
                 place = pair * 2 + inner
-                whole = half * PLACES + place
-                near = table[MISC + 3, whole] > 0
-                rows = jnp.where(near, near_recv[whole], far_recv[whole])[6:12]
+                rows = far_recv[half * PLACES + place][6:12]
                 last_tiles[half][place] = tile(rows, own_side(HALVES + half, place))
             return 0
 
         lax.fori_loop(0, PLACES // 2, build_last, 0)
 
     def build_rest(apart, _):
-        rows = far_recv[rest[6, apart] & (DEVICES - 1)][6:12]
-        rest_tiles[apart] = tile(rows, features[rest[4, apart] & (BLOCKS - 1)])
+        own = features[rest[4, apart] & (BLOCKS - 1)]
+        rest_tiles[apart] = tile(shape_came[apart][:6], own)
         return 0
-
-    lax.fori_loop(0, RANKS, build_rest, 0)
 
     def accumulate(values_ref, tiles_ref, rows, base, first):
         tasks = values_ref.shape[0]
@@ -715,6 +772,9 @@
         for kind, each in rounds:
             left(kind, send, PEERS * each)
 
+        if sweep == 0:
+            geometry_came()
+            lax.fori_loop(0, RANKS, build_rest, 0)
         passed_came(sweep)
         for apart in range(RANKS):
             for piece in range(PIECES):
@@ -753,6 +813,8 @@
     last_tiles = pltpu.VMEM((PLACES, BLK, BLK), jnp.bfloat16)
     message = pltpu.VMEM((DEVICES, 16, BLK), jnp.float32)
     lent = pltpu.VMEM((DEVICES, ROWS, BLK), jnp.bfloat16)
+    shapes = pltpu.VMEM((RANKS, 8, BLK), jnp.float32)
+    all_shapes = pltpu.VMEM((DEVICES, 8, BLK), jnp.float32)
     passed = pltpu.VMEM((RELAYS, ROWS, BLK), jnp.bfloat16)
     return pl.pallas_call(
         fused_kernel,
@@ -774,8 +836,8 @@
             pltpu.VMEM((PLACES * 2, BANDS, BLK), jnp.float32),
             pltpu.VMEM((DEVICES * 2, BANDS, BLK), jnp.bfloat16),
             pltpu.VMEM((DEVICES, BANDS, BLK), jnp.bfloat16),
-            message,
-            message,
+            all_shapes,
+            all_shapes,
             message,
             message,
             pltpu.VMEM((DEVICES, BLK), jnp.float32),
@@ -789,11 +851,12 @@
         + [values] * (SWEEPS * HALVES)
         + [last_values] * (SWEEPS * HALVES)
         + [passed, lent, lent, lent, passed, passed]
+        + [shapes, all_shapes, all_shapes, shapes]
         + [
             pltpu.VMEM((RANKS, BLK, BLK), jnp.bfloat16),
             pltpu.VMEM((RANKS, BANDS, BLK), jnp.bfloat16),
-            pltpu.SemaphoreType.DMA((11,)),
-            pltpu.SemaphoreType.DMA((22,)),
+            pltpu.SemaphoreType.DMA((13,)),
+            pltpu.SemaphoreType.DMA((26,)),
             pltpu.SemaphoreType.DMA((3,)),
         ],
         compiler_params=pltpu.CompilerParams(

time: 205 us -> 215 us (1.049)
  Pallas kernels: 202 us -> 210 us
    pallas_call x1, Pallas kernels: 202 us -> 210 us  [fused(): pl.pallas_call(fused_kernel, in_specs=[vmem] * 10, out_specs=[vmem, smem]...]
where the time goes in v2:
time: 215 us; the launch traced here: 214 us
  Pallas kernels  210 us (98%)
    pallas_call x1, Pallas kernels, fused(): pl.pallas_call(fused_kernel, in_specs=[vmem] * 10, out_specs=[vmem, smem]...  210 us

profile of v2, /device:TPU:1, one launch (start us, length us, event | category | flops | bytes accessed | tf_op | source)
XLA Modules:
  0.0 213.8 jit_solution(9766411737479152455)
XLA Ops:
  0.0 210.4 %fused.1 = (f32[64,4096]{1,0:T(8,128)}, s32[1,1]{1,0:T(1,128)}) custom-call(s32[8,128]{1,0:T(8,128)} %constant.8.clone.steps, s32[1,128]{1,0:T(1,128)} %bitcast.139, s32[1,128]{1,0:T(1,128)} %bitcast.144, s32[1,128]{1,0:T(1,128)} %bitcast.142, f32[64,4096]{1,0:T(8,128)} %emission.1, f32[1,4096]{1,0:T(1,128)} %bitcast.88, s32[1,4096]{1,0:T(1,128)} %bitcast.87, ...), custom_call_target="tpu_custom_call" | custom-call | tf_op jit(solution)/shard_map/fused/pallas_call | solution.py:819
  211.0 1.8 conditional.1
  211.1 1.7 add.69
  212.8 0.0 copy-start
  212.8 1.0 copy-done
Async XLA Ops:
  212.8 1.0 copy-start

commit v3 on v1

--- a/solution.py
+++ b/solution.py
@@ -464,6 +464,14 @@
 
         return lambda place: last_send.at[place], target
 
+    def at_places(act):
+        def step(group, _):
+            for inner in range(8):
+                act(group * 8 + inner)
+            return 0
+
+        lax.fori_loop(0, DEVICES // 8, step, 0)
+
     def near_index(place, slot):
         return names[slot, place] & (BLOCKS - 1)
 
@@ -471,11 +479,10 @@
         return table[MISC + row, BACK[place]] & (BLOCKS - 1)
 
     def pack_near_values():
-        def pack(place, _):
+        def pack(place):
             send[place * 2] = scaled[near_index(place, 0)]
-            return 0
-
-        lax.fori_loop(0, DEVICES, pack, 0)
+
+        at_places(pack)
 
     def pack_far_values():
         for place in range(DEVICES):
@@ -552,20 +559,19 @@
     to_names.wait()
     lane = lax.broadcasted_iota(jnp.int32, (4, BLK), 1)
 
-    def pack_near(place, _):
+    def pack_near(place):
         first, second = names[0, place], names[1, place]
         codes = jnp.where(lane == 0, first, jnp.where(lane == 1, second, 0)).astype(jnp.float32)
         rows = [geometry[near_index(place, slot)][:6] for slot in range(2)]
         near_send[place] = jnp.concatenate(rows + [codes], 0)
-        return 0
-
-    lax.fori_loop(0, DEVICES, pack_near, 0)
+
+    at_places(pack_near)
     near_recv[PEERS] = near_send[PEERS]
+    pl.semaphore_wait(barrier, PEERS)
+    exchange(0, lambda place: near_send.at[place], lambda place: near_recv.at[place], False)
     for block in range(BLOCKS):
         lanes = pl.ds(block * BLK, BLK)
         scaled[block] = (emission[:, lanes] * areas[:, lanes]).astype(jnp.bfloat16)
-    pl.semaphore_wait(barrier, PEERS)
-    exchange(0, lambda place: near_send.at[place], lambda place: near_recv.at[place], False)
     pack_near_values()
     exchange(2, *firsts(0, 0, 1))
 
@@ -589,11 +595,10 @@
 
     all_of(0, near_recv.at[pl.ds(0, PEERS)]).wait_recv()
 
-    def collect_asked(place, _):
+    def collect_asked(place):
         asked_rows[pl.ds(place, 1)] = near_recv[place, 12:13]
-        return 0
-
-    lax.fori_loop(0, DEVICES, collect_asked, 0)
+
+    at_places(collect_asked)
     asked = asked_rows[...].T[:8].astype(jnp.int32)
     route(asked, name_table[2:5], table_rows)
     to_table = pltpu.make_async_copy(table_rows, table, table_sem.at[0])
@@ -632,11 +637,10 @@
 
     all_of(1, far_recv.at[pl.ds(0, PEERS)]).wait_recv()
 
-    def collect_crowded(place, _):
+    def collect_crowded(place):
         asked_rows[pl.ds(place, 1)] = far_recv[place, 12:13]
-        return 0
-
-    lax.fori_loop(0, DEVICES, collect_crowded, 0)
+
+    at_places(collect_crowded)
     crowded = asked_rows[...].T[:1]
     shift = (chip // PIECES).astype(jnp.float32)
     route_rest(crowded, asked, name_table[2:5], shift, rest_rows)

time: 205 us -> 205 us (level)
  no operation moved by 1% of the time
where the time goes in v3:
time: 205 us; the launch traced here: 204 us
  Pallas kernels  201 us (98%)
    pallas_call x1, Pallas kernels, fused(): pl.pallas_call(fused_kernel, in_specs=[vmem] * 10, out_specs=[vmem, smem]...  201 us

profile of v3, /device:TPU:1, one launch (start us, length us, event | category | flops | bytes accessed | tf_op | source)
XLA Modules:
  0.0 204.4 jit_solution(16854104572073495338)
XLA Ops:
  0.0 200.9 %fused.1 = (f32[64,4096]{1,0:T(8,128)}, s32[1,1]{1,0:T(1,128)}) custom-call(s32[8,128]{1,0:T(8,128)} %constant.8.clone.steps, s32[1,128]{1,0:T(1,128)} %bitcast.139, s32[1,128]{1,0:T(1,128)} %bitcast.144, s32[1,128]{1,0:T(1,128)} %bitcast.142, f32[64,4096]{1,0:T(8,128)} %emission.1, f32[1,4096]{1,0:T(1,128)} %bitcast.88, s32[1,4096]{1,0:T(1,128)} %bitcast.87, ...), custom_call_target="tpu_custom_call" | custom-call | tf_op jit(solution)/shard_map/fused/pallas_call | solution.py:761
  201.5 1.9 conditional.1
  201.7 1.7 add.69
  203.4 0.0 copy-start
  203.4 1.0 copy-done
Async XLA Ops:
  203.4 1.0 copy-start
